TPU v7x, 32 devices: a whole 2x2x4 slice. The times are simulated.
32 devices in a mesh: rep: 8 (over y, x, core), grp: 4 (over z).
Axes of the slice: x: 2, y: 2, z: 4, core: 2. Of those that a mesh axis runs over, the one named last changes fastest.
Arguments:
- tokens: bfloat16 [4096, 1536], P(('rep', 'grp')), may hold values from -6 to 6
- attn_gain: bfloat16 [1536], P('grp'), may hold values from 0.5 to 1.5
- query_key_value_weight: bfloat16 [1536, 2560], P('grp'), may hold values from -0.15625 to 0.15625
- attn_proj: bfloat16 [1536, 1536], P('grp'), may hold values from -1.25 to 1.25
- mlp_gain: bfloat16 [1536], P('grp'), may hold values from 0.5 to 1.5
- w_router: bfloat16 [1536, 16], P('grp'), may hold values from -0.078125 to 0.078125
- w_gate_up: bfloat16 [1536, 16, 1024], P('grp'), may hold values from -0.15625 to 0.15625
- w_down: bfloat16 [1536, 16, 512], P('grp'), may hold values from -1 to 1
- prefix_len: int32 [32], P(('rep', 'grp')), may hold values from 0 to 128
- expert_ids: int32 [4096, 8], P(('rep', 'grp')), may hold values from 0 to 15, all different within a row
- priority: int32 [32, 1024], P(('rep', 'grp')), may hold values from 0 to 1023, each once within a row
- cotangent: bfloat16 [4096, 1536], P(('rep', 'grp')), may hold values from -6 to 6
Outputs:
- output: bfloat16 [4096, 1536], P(('rep', 'grp'))
- grad_tokens: float32 [4096, 1536], P(('rep', 'grp'))
- grad_attn_gain: float32 [1536], P('grp')
- grad_w_qkv: float32 [1536, 2560], P('grp')
- grad_attn_proj: float32 [1536, 1536], P('grp')
- grad_mlp_gain: float32 [1536], P('grp')
- grad_w_router: float32 [1536, 16], P('grp')
- grad_w_gate_up: float32 [1536, 16, 1024], P('grp')
- grad_w_down: float32 [1536, 16, 512], P('grp')
Inputs may be any that keep to these rules, and one draw needn't show every extreme that they name: `prefix_len`: positions below a sequence's prefix length attend to one another in both directions. `expert_ids`: the 8 experts of a token are different. `priority`: each row holds every number of 0 to 1023 once.
All inputs are finite; a program needn't handle non-finite values.
Results may differ from a plain program's by a relative error of at most 0.015.
Values may be sent and summed in bfloat16 or wider, within the bound.
A program may use at most 576 MiB of HBM per device.

v0:
```python
import jax
import jax.numpy as jnp
from jax import lax
from jax.sharding import PartitionSpec as P

QUERY_HEADS = 24
KEY_VALUE_HEADS = 8
HEAD_WIDTH = 64
HID = 512
EXPERTS = 16
CAP = 72
EPS = 1e-05
BF = jnp.bfloat16
F32 = jnp.float32
QPK = QUERY_HEADS // KEY_VALUE_HEADS
BIG = 1 << 20


def dot(a, b):
    return jnp.dot(a, b, preferred_element_type=F32)


def rope_tables(length):
    half = HEAD_WIDTH // 2
    position = jnp.arange(length, dtype=F32)[:, None]
    inverse_freq = 10000.0 ** (-jnp.arange(half, dtype=F32) * 2.0 / HEAD_WIDTH)
    angles = position * inverse_freq[None, :]
    return (jnp.cos(angles), jnp.sin(angles))


def rotate(v, cos, sin):
    half = HEAD_WIDTH // 2
    a, b = (v[..., :half], v[..., half:])
    return jnp.concatenate([a * cos - b * sin, b * cos + a * sin], axis=-1)


def routing(expert_ids, priority, logits):
    seq, top = expert_ids.shape
    choose = expert_ids[:, :, None] == jnp.arange(EXPERTS, dtype=jnp.int32)[None, None, :]
    chosen = jnp.any(choose, axis=1)
    rank_of = jnp.sum(jnp.where(choose, priority.reshape(seq, top)[:, :, None], 0), axis=1)
    rank_of = jnp.where(chosen, rank_of, BIG)
    slot = jnp.sum((rank_of[None, :, :] < rank_of[:, None, :]).astype(jnp.int32), axis=1)
    kept = chosen & (slot < CAP)
    top_logit = jnp.max(jnp.where(chosen, logits, -jnp.inf), axis=1, keepdims=True)
    gate_exp = jnp.where(chosen, jnp.exp(jnp.where(chosen, logits - top_logit, 0.0)), 0.0)
    gates = gate_exp / jnp.sum(gate_exp, axis=1, keepdims=True)
    return (gates, kept)


def shards(
    reps,
    grps,
    tokens,
    attn_gain,
    query_key_value_weight,
    attn_proj,
    mlp_gain,
    w_router,
    w_gate_up,
    w_down,
    prefix_len,
    expert_ids,
    priority,
    cotangent,
):
    seq, width = tokens.shape
    own = width // grps
    local_experts = EXPERTS // grps
    heads = KEY_VALUE_HEADS
    groups = None if reps == heads else [list(range(i, i + heads)) for i in range(0, reps, heads)]
    rep, grp = (lax.axis_index("rep"), lax.axis_index("grp"))
    head = lax.rem(rep, heads)
    qw, hw = (QPK * HEAD_WIDTH, HEAD_WIDTH)
    q_all = QUERY_HEADS * HEAD_WIDTH
    small = jnp.concatenate([attn_gain[:, None], mlp_gain[:, None], w_router], axis=1)
    small = lax.all_gather(small, "grp", axis=0, tiled=True)
    gain_one, gain_two = (small[:, 0].astype(F32)[None, :], small[:, 1].astype(F32)[None, :])
    router = small[:, 2:]
    qkv_cols = jnp.concatenate(
        [
            lax.dynamic_slice_in_dim(query_key_value_weight, head * qw, qw, 1),
            lax.dynamic_slice_in_dim(query_key_value_weight, q_all + head * hw, hw, 1),
            lax.dynamic_slice_in_dim(query_key_value_weight, q_all + heads * hw + head * hw, hw, 1),
        ],
        axis=1,
    )
    qkv_head = lax.all_gather(qkv_cols, "grp", axis=0, tiled=True)
    row = head * qw + jnp.arange(qw)
    mine = row // own == grp
    proj_rows = jnp.where(
        mine[:, None], jnp.take(attn_proj, jnp.where(mine, row - grp * own, 0), axis=0), 0
    )
    proj_head = lax.psum(proj_rows, "grp")
    piece = own // reps
    gu_piece = lax.dynamic_slice_in_dim(w_gate_up, rep * piece, piece, 0)
    dn_piece = lax.dynamic_slice_in_dim(w_down, rep * piece, piece, 0)
    both = jnp.concatenate([gu_piece, dn_piece], axis=2)
    both = both.reshape(piece, grps, local_experts, 3 * HID).transpose(1, 2, 0, 3)
    both = lax.all_to_all(both, "grp", 0, 0, tiled=True)
    both = lax.all_gather(both, "rep", axis=0, tiled=False)
    both = both.transpose(2, 1, 0, 3, 4).reshape(local_experts, width, 3 * HID)
    wgu, wdn = (both[:, :, : 2 * HID], both[:, :, 2 * HID :])
    tokens_f = tokens.astype(F32)
    inverse_one = lax.rsqrt(jnp.mean(tokens_f * tokens_f, axis=1, keepdims=True) + EPS)
    normed_one = tokens_f * inverse_one
    act_one = (normed_one * gain_one).astype(BF)
    act_plane = lax.all_gather(act_one, "rep", axis=0, tiled=True, axis_index_groups=groups)
    prefix_plane = lax.all_gather(prefix_len, "rep", axis=0, tiled=True, axis_index_groups=groups)
    cos, sin = rope_tables(seq)
    projected = dot(act_plane, qkv_head).reshape(heads, seq, QPK + 2, HEAD_WIDTH)
    cos_b, sin_b = (cos[None, :, None, :], sin[None, :, None, :])
    turned = rotate(projected[:, :, : QPK + 1], cos_b, sin_b).astype(BF)
    query = turned[:, :, :QPK]
    key = turned[:, :, QPK]
    value = projected[:, :, QPK + 1].astype(BF)
    scale = HEAD_WIDTH ** (-0.5)
    row_pos, col_pos = (jnp.arange(seq)[:, None], jnp.arange(seq)[None, :])
    allowed = (col_pos <= row_pos)[None] | (col_pos[None] < prefix_plane[:, None, None])
    scores = jnp.einsum("bsgd,btd->bgst", query, key, preferred_element_type=F32) * scale
    scores = jnp.where(allowed[:, None], scores, -1e30)
    exps = jnp.exp(scores - jnp.max(scores, axis=-1, keepdims=True))
    probs = exps / jnp.sum(exps, axis=-1, keepdims=True)
    probs_low = probs.astype(BF)
    attended = jnp.einsum("bgst,btd->bsgd", probs_low, value, preferred_element_type=F32)
    attended = attended.astype(BF).reshape(heads * seq, qw)
    part = dot(attended, proj_head).astype(BF)
    part = lax.psum_scatter(part, "rep", scatter_dimension=0, tiled=True, axis_index_groups=groups)
    residual = tokens_f + part.astype(F32)
    inverse_two = lax.rsqrt(jnp.mean(residual * residual, axis=1, keepdims=True) + EPS)
    normed_two = residual * inverse_two
    act_two = (normed_two * gain_two).astype(BF)
    gates, kept = routing(expert_ids, priority, dot(act_two, router))
    dy_all = lax.all_gather(cotangent, "grp", axis=0, tiled=True)
    x_all = lax.all_gather(act_two, "grp", axis=0, tiled=True)
    weight = lax.all_gather(jnp.where(kept, gates, 0.0), "grp", axis=0, tiled=True)
    weight = lax.dynamic_slice_in_dim(weight, grp * local_experts, local_experts, 1).T[:, :, None]
    gate_up = jnp.einsum("td,edh->eth", x_all, wgu, preferred_element_type=F32)
    g, u = (gate_up[..., :HID], gate_up[..., HID:])
    sig = jax.nn.sigmoid(g)
    silu = g * sig
    hidden = silu * u
    hidden_w = (hidden * weight).astype(BF)
    back = jnp.einsum("td,edh->eth", dy_all, wdn, preferred_element_type=F32)
    grad_gate_part = jnp.sum(back * hidden, axis=2)
    grad_hidden = back * weight
    ggu = jnp.concatenate(
        [grad_hidden * u * sig * (1.0 + g * (1.0 - sig)), grad_hidden * silu], axis=2
    ).astype(BF)
    out_part = jnp.einsum("eth,edh->td", hidden_w, wdn, preferred_element_type=F32).astype(BF)
    gact_part = jnp.einsum("eth,edh->td", ggu, wgu, preferred_element_type=F32).astype(BF)
    gact = lax.psum_scatter(gact_part, "grp", scatter_dimension=0, tiled=True).astype(F32)
    grad_gates = lax.all_to_all(grad_gate_part.T, "grp", 0, 1, tiled=True)
    grad_gates = jnp.where(kept, grad_gates, 0.0)
    gw_gu = jnp.einsum("td,eth->edh", x_all, ggu, preferred_element_type=F32).astype(BF)
    gw_dn = jnp.einsum("td,eth->edh", dy_all, hidden_w, preferred_element_type=F32).astype(BF)
    gw = jnp.concatenate([gw_gu, gw_dn], axis=2)
    gw = gw.reshape(local_experts, grps, reps, piece, 3 * HID).transpose(2, 1, 3, 0, 4)
    gw = gw.reshape(reps * grps * piece, EXPERTS // grps * 3 * HID)
    gw = lax.psum_scatter(gw, "rep", scatter_dimension=0, tiled=True)
    gw = gw.reshape(grps, piece, local_experts, 3 * HID)
    gw = lax.all_to_all(gw, "grp", 0, 0, tiled=True)
    gw = gw.transpose(1, 0, 2, 3).reshape(piece, EXPERTS, 3 * HID)
    gw = lax.all_gather(gw, "rep", axis=0, tiled=True)
    grad_gu = gw[:, :, : 2 * HID].astype(F32)
    grad_dn = gw[:, :, 2 * HID :].astype(F32)
    out = lax.psum_scatter(out_part, "grp", scatter_dimension=0, tiled=True).astype(F32)
    output = (residual + out).astype(BF)
    grad_logits = (
        gates * (grad_gates - jnp.sum(gates * grad_gates, axis=1, keepdims=True))
    ).astype(BF)
    gact = gact + dot(grad_logits, router.T)
    router_term = dot(act_two.T, grad_logits)
    gain_two_term = jnp.sum(gact * normed_two, axis=0)
    scaled = gact * gain_two
    dy = cotangent.astype(F32)
    grad_residual = dy + inverse_two * (
        scaled - normed_two * jnp.mean(scaled * normed_two, axis=1, keepdims=True)
    )
    gres_low = grad_residual.astype(BF)
    gres_plane = lax.all_gather(gres_low, "rep", axis=0, tiled=True, axis_index_groups=groups)
    proj_term = dot(attended.T, gres_plane)
    grad_att = dot(gres_plane, proj_head.T).astype(BF).reshape(heads, seq, QPK, HEAD_WIDTH)
    grad_value = jnp.einsum("bgst,bsgd->btd", probs_low, grad_att, preferred_element_type=F32)
    grad_probs = jnp.einsum("bsgd,btd->bgst", grad_att, value, preferred_element_type=F32)
    grad_scores = (
        probs * (grad_probs - jnp.sum(probs * grad_probs, axis=-1, keepdims=True))
    ).astype(BF)
    grad_query = jnp.einsum("bgst,btd->bsgd", grad_scores, key, preferred_element_type=F32) * scale
    grad_key = jnp.einsum("bgst,bsgd->btd", grad_scores, query, preferred_element_type=F32) * scale
    turned_back = rotate(jnp.concatenate([grad_query, grad_key[:, :, None]], axis=2), cos_b, -sin_b)
    gproj = jnp.concatenate([turned_back, grad_value[:, :, None]], axis=2).astype(BF)
    gproj = gproj.reshape(heads * seq, qw + 2 * hw)
    qkv_term = dot(act_plane.T, gproj)
    gact_one = dot(gproj, qkv_head.T).astype(BF)
    gact_one = lax.psum_scatter(
        gact_one, "rep", scatter_dimension=0, tiled=True, axis_index_groups=groups
    ).astype(F32)
    gain_one_term = jnp.sum(gact_one * normed_one, axis=0)
    scaled_one = gact_one * gain_one
    grad_tokens = grad_residual + inverse_one * (
        scaled_one - normed_one * jnp.mean(scaled_one * normed_one, axis=1, keepdims=True)
    )
    qkv_own = lax.psum_scatter(qkv_term.astype(BF), "grp", scatter_dimension=0, tiled=True)
    proj_sum = lax.psum(proj_term.astype(BF), "grp")
    if groups is not None:
        across = [[i + heads * j for j in range(reps // heads)] for i in range(heads)]
        qkv_own = lax.psum(qkv_own, "rep", axis_index_groups=across)
        proj_sum = lax.psum(proj_sum, "rep", axis_index_groups=across)
    qkv_own = lax.all_gather(qkv_own, "rep", axis=0, tiled=False, axis_index_groups=groups)
    qkv_own = qkv_own.astype(F32)
    grad_qkv = jnp.concatenate(
        [
            qkv_own[:, :, lo:hi].transpose(1, 0, 2).reshape(own, -1)
            for lo, hi in ((0, qw), (qw, qw + hw), (qw + hw, qw + 2 * hw))
        ],
        axis=1,
    )
    proj_all = lax.all_gather(proj_sum, "rep", axis=0, tiled=True, axis_index_groups=groups)
    grad_proj = lax.dynamic_slice_in_dim(proj_all, grp * own, own, 0).astype(F32)
    terms = jnp.concatenate([gain_one_term[:, None], gain_two_term[:, None], router_term], axis=1)
    terms = lax.psum(lax.psum_scatter(terms, "grp", scatter_dimension=0, tiled=True), "rep")
    return (
        output,
        grad_tokens,
        terms[:, 0],
        grad_qkv,
        grad_proj,
        terms[:, 1],
        terms[:, 2:],
        grad_gu,
        grad_dn,
    )


def solution(mesh):
    tok, par = (("rep", "grp"), "grp")
    in_specs = (
        P(tok, None),
        P(par),
        P(par, None),
        P(par, None),
        P(par),
        P(par, None),
        P(par, None, None),
        P(par, None, None),
        P(tok),
        P(tok, None),
        P(tok, None),
        P(tok, None),
    )
    out_specs = (
        P(tok, None),
        P(tok, None),
        P(par),
        P(par, None),
        P(par, None),
        P(par),
        P(par, None),
        P(par, None, None),
        P(par, None, None),
    )
    reps, grps = (mesh.shape["rep"], mesh.shape["grp"])

    def body(*args):
        return shards(reps, grps, *args)

    return jax.shard_map(body, mesh=mesh, in_specs=in_specs, out_specs=out_specs, check_vma=False)
```

profile of v0, /device:TPU:0, one launch (start us, length us, event | category | flops | bytes accessed | tf_op | source)
XLA Modules:
  0.0 1020.9 jit_solution(18360861975439800956)
XLA Ops:
  11.4 14.9 %all_gather.42 = bf16[1536,18]{0,1:T(8,128)(2,1)S(1)} all-gather(bf16[384,18]{0,1:T(8,128)(2,1)S(1)} %pad_maximum_fusion.17), channel_id=1, replica_groups=mesh['rep'=8,'grp'=4] {'grp'}, dimensions={0}, use_global_device_ids=true | all-gather | bytes 69120 | tf_op jit(solution)/shard_map/all_gather | solution.py:77
  32.6 8.0 all-reduce
  43.2 30.3 %all_gather.44 = bf16[1536,320]{1,0:T(8,128)(2,1)S(1)} all-gather(bf16[384,320]{1,0:T(8,128)(2,1)S(1)} %pad_maximum_fusion.9), channel_id=1, replica_groups=mesh['rep'=8,'grp'=4] {'grp'}, dimensions={0}, use_global_device_ids=true | all-gather | bytes 1228800 | tf_op jit(solution)/shard_map/all_gather | solution.py:88
  89.5 56.0 %all_to_all.29 = bf16[4,4,48,1536]{3,2,1,0:T(8,128)(2,1)} all-to-all(bf16[4,4,48,1536]{3,2,1,0:T(8,128)(2,1)S(1)} %bitcast.193), channel_id=1, replica_groups=mesh['rep'=8,'grp'=4] {'grp'}, dimensions={0} | all-to-all | bytes 4718592 | tf_op jit(solution)/shard_map/all_to_all | solution.py:100
  154.7 88.9 %all-gather.23.cloned.1.call-done = bf16[32,4,48,1536]{3,2,1,0:T(8,128)(2,1)} async-done(((bf16[4,4,48,1536]{3,2,1,0:T(8,128)(2,1)}), bf16[32,4,48,1536]{3,2,1,0:T(8,128)(2,1)}) %all-gather.23.cloned.1.call-update) | async-done | bytes 18874384 | tf_op jit(solution)/shard_map/all_gather | solution.py:101
  243.6 17.1 %copy.160 = bf16[4,4,8,48,1536]{4,3,2,1,0:T(8,128)(2,1)} copy(bf16[4,4,8,48,1536]{4,3,0,1,2:T(8,128)(2,1)} %bitcast.188) | data formatting | bytes 37748736 | tf_op jit(solution)/shard_map/transpose | solution.py:102
  260.8 22.1 %all-gather.13.cloned.1.call-done = bf16[512,1536]{1,0:T(8,128)(2,1)} async-done(((bf16[128,1536]{1,0:T(8,128)(2,1)}), bf16[512,1536]{1,0:T(8,128)(2,1)}) %all-gather.13.cloned.1.call-update) | async-done | bytes 1572880 | tf_op jit(solution)/shard_map/all_gather | solution.py:135
  282.8 12.3 %fusion.18 = f32[4,512,1024]{1,2,0:T(8,128)} fusion(bf16[4,1536,1536]{2,1,0:T(8,128)(2,1)} %bitcast.184, bf16[512,1536]{1,0:T(8,128)(2,1)} %all-gather.13.cloned.1.call-done), kind=kOutput, calls=%fused_computation.31 | convolution fusion | flops 6442450944 | bytes 22544384 | tf_op jit(solution)/shard_map/td,edh->eth/dot_general | solution.py:138
  295.2 25.2 %all-gather.15.cloned.1.call-done = bf16[512,1536]{1,0:T(8,128)(2,1)} async-done(((bf16[128,1536]{1,0:T(8,128)(2,1)}), bf16[512,1536]{1,0:T(8,128)(2,1)}) %all-gather.15.cloned.1.call-update) | async-done | bytes 1572880 | tf_op jit(solution)/shard_map/all_gather | solution.py:134
  320.3 12.6 %fusion.10 = (f32[4,512]{1,0:T(4,128)}, f32[4,512,512]{2,1,0:T(8,128)}) fusion(f32[4,512,1024]{1,2,0:T(8,128)} %fusion.18, bf16[512,1536]{1,0:T(8,128)(2,1)} %all-gather.15.cloned.1.call-done, bf16[4,1536,1536]{2,1,0:T(8,128)(2,1)} %bitcast.185), kind=kOutput, calls=%fused_computation.19 | convolution fusion | flops 3228563456 | bytes 20455424 | tf_op jit(solution)/shard_map/td,edh->eth/dot_general | solution.py:144
  341.8 13.5 %all_gather.49 = f32[512,16]{0,1:T(8,128)S(1)} all-gather(f32[128,16]{0,1:T(8,128)S(1)} %get-tuple-element.80), channel_id=1, replica_groups=mesh['rep'=8,'grp'=4] {'grp'}, dimensions={0}, use_global_device_ids=true | all-gather | bytes 40960 | tf_op jit(solution)/shard_map/all_gather | solution.py:136
  355.3 6.9 multiply_convert_fusion.1
  364.2 10.8 %fusion.24 = bf16[512,1536]{1,0:T(8,128)(2,1)} fusion(bf16[4,1536,1536]{2,1,0:T(8,128)(2,1)} %bitcast.186, bf16[4,512,512]{1,2,0:T(8,128)(2,1)S(1)} %get-tuple-element.65, bf16[4,512,512]{1,2,0:T(8,128)(2,1)S(1)} %get-tuple-element.64), kind=kOutput, calls=%fused_computation.33 | convolution fusion | flops 6451625984 | bytes 18350080 | tf_op jit(solution)/shard_map/eth,edh->td/dot_general | solution.py:151
  375.1 33.6 %reduce-scatter.14.cloned.1.call-done = bf16[128,1536]{1,0:T(8,128)(2,1)} async-done(((bf16[512,1536]{1,0:T(8,128)(2,1)}), bf16[128,1536]{1,0:T(8,128)(2,1)}) %reduce-scatter.14.cloned.1.call-update) | async-done | bytes 393232 | tf_op jit(solution)/shard_map/reduce_scatter | solution.py:152
  412.3 31.3 %all-gather.17.cloned.1.call-done = bf16[1024,1536]{1,0:T(8,128)(2,1)} async-done(((bf16[128,1536]{1,0:T(8,128)(2,1)}), bf16[1024,1536]{1,0:T(8,128)(2,1)}) %all-gather.17.cloned.1.call-update) | async-done | bytes 3145744 | tf_op jit(solution)/shard_map/all_gather | solution.py:181
  461.6 7.0 convert_bitcast_fusion
  468.6 10.6 %fusion.5 = bf16[4,1536,1024]{1,2,0:T(8,128)(2,1)} fusion(bf16[4,512,512]{1,2,0:T(8,128)(2,1)S(1)} %copy-done.15, bf16[4,512,512]{1,2,0:T(8,128)(2,1)S(1)} %copy-done.13, bf16[512,1536]{1,0:T(8,128)(2,1)S(1)} %copy-done.34), kind=kOutput, calls=%fused_computation.9 | convolution fusion | flops 6457131008 | bytes 18350080 | tf_op jit(solution)/shard_map/td,eth->edh/dot_general | solution.py:155
  480.9 20.9 %pad_maximum_fusion = bf16[4,1536,1536]{1,2,0:T(8,128)(2,1)} fusion(bf16[4,1536,512]{1,2,0:T(8,128)(2,1)} %convert_bitcast_fusion, bf16[4,1536,1024]{1,2,0:T(8,128)(2,1)} %fusion.5), kind=kLoop, calls=%fused_computation.2 | loop fusion | flops 37748736 | bytes 37748736 | tf_op jit(solution)/shard_map/concatenate | solution.py:157
  501.8 24.7 %copy.178 = bf16[4,1536,1536]{2,1,0:T(8,128)(2,1)} copy(bf16[4,1536,1536]{1,2,0:T(8,128)(2,1)} %pad_maximum_fusion) | data formatting | bytes 37748736 | tf_op jit(solution)/shard_map/concatenate | solution.py:157
  526.5 21.6 %copy.179 = bf16[8,4,48,4,1536]{4,3,2,1,0:T(4,128)(2,1)S(1)} copy(bf16[8,4,48,4,1536]{4,2,0,1,3:T(8,128)(2,1)} %bitcast.182) | data formatting | bytes 37748736 | tf_op jit(solution)/shard_map/transpose | solution.py:158
  548.1 9.7 copy.207
  559.4 7.4 fusion.21
  572.7 111.4 %reduce-scatter.20.cloned.1.call-done = bf16[192,6144]{1,0:T(8,128)(2,1)} async-done(((bf16[1536,6144]{1,0:T(8,128)(2,1)}), bf16[192,6144]{1,0:T(8,128)(2,1)}) %reduce-scatter.20.cloned.1.call-update) | async-done | bytes 2359312 | tf_op jit(solution)/shard_map/reduce_scatter | solution.py:160
  687.7 84.3 %all_to_all.30 = bf16[4,48,4,1536]{3,2,1,0:T(4,128)(2,1)S(1)} all-to-all(bf16[4,48,4,1536]{3,2,1,0:T(4,128)(2,1)S(1)} %reshape.284), channel_id=1, replica_groups=mesh['rep'=8,'grp'=4] {'grp'}, dimensions={0} | all-to-all | bytes 4718592 | tf_op jit(solution)/shard_map/all_to_all | solution.py:162
  780.0 23.5 %psum.22 = f32[384,18]{0,1:T(8,128)S(1)} all-reduce(f32[384,18]{0,1:T(8,128)} %reduce-scatter.18.cloned.1.call-done), channel_id=1, replica_groups=mesh['rep'=8,'grp'=4] {'rep'}, use_global_device_ids=true, to_apply=%region_22.23 | all-reduce | flops 6912 | bytes 55296 | tf_op jit(solution)/shard_map/psum | solution.py:222
  814.5 5.5 copy.181
  820.0 29.4 %all-gather.19.cloned.1.call-done = bf16[1536,1536]{1,0:T(8,128)(2,1)} async-done(((bf16[192,1536]{1,0:T(8,128)(2,1)}), bf16[1536,1536]{1,0:T(8,128)(2,1)}) %all-gather.19.cloned.1.call-update) | async-done | bytes 4718608 | tf_op jit(solution)/shard_map/all_gather | solution.py:219
  852.4 98.3 %all-gather.21.cloned.1.call-done = bf16[384,16,1536]{2,0,1:T(8,128)(2,1)} async-done(((bf16[48,16,1536]{2,0,1:T(8,128)(2,1)}), bf16[384,16,1536]{2,0,1:T(8,128)(2,1)}) %all-gather.21.cloned.1.call-update) | async-done | bytes 18874384 | tf_op jit(solution)/shard_map/all_gather | solution.py:164
  950.7 9.3 slice_convert_fusion.1
  960.0 16.6 %copy.183 = f32[384,16,512]{2,1,0:T(8,128)} copy(f32[384,16,512]{2,0,1:T(8,128)} %slice_convert_fusion.1) | data formatting | bytes 25165824
  976.6 7.4 slice_convert_fusion
  984.0 29.1 %copy.182 = f32[384,16,1024]{2,1,0:T(8,128)} copy(f32[384,16,1024]{2,0,1:T(8,128)S(1)} %slice_convert_fusion) | data formatting | bytes 50331648
  (209 shorter events, 103.1 us)
Async XLA Ops:
  8.0 20.4 %copy-start = (bf16[384,1536]{1,0:T(8,128)(2,1)S(1)}, bf16[384,1536]{1,0:T(8,128)(2,1)}, u32[]{:S(2)}) copy-start(bf16[384,1536]{1,0:T(8,128)(2,1)} %param.15) | copy-start | bytes 3538948
  8.0 65.7 %all-gather.11.cloned.1.call-start = ((), (), s32[]{:S(2)}) async-start(), calls=%async_computation.10 | async-start | bytes 3538944 | tf_op jit(solution)/shard_map/all_gather | solution.py:108
  9.3 19.0 %copy-start.27 = (f32[128]{0:T(128)}, f32[128]{0:T(128)S(1)}, u32[]{:S(2)}) copy-start(f32[128]{0:T(128)S(1)} %add_rsqrt_fusion.1) | copy-start | bytes 1540
  28.3 53.1 %all-reduce.4.cloned.1.call-start = ((), (), s32[]{:S(2)}) async-start(), calls=%async_computation.11 | async-start | bytes 1179648 | tf_op jit(solution)/shard_map/psum | solution.py:94
  30.5 115.1 %reduce-scatter.10.cloned.1.call-start = ((), (), s32[]{:S(2)}) async-start(), calls=%async_computation.12 | async-start | bytes 3538944 | tf_op jit(solution)/shard_map/reduce_scatter | solution.py:128
  85.2 158.5 %all-gather.23.cloned.1.call-start = ((), (), s32[]{:S(2)}) async-start(), calls=%async_computation.24 | async-start | bytes 21233664 | tf_op jit(solution)/shard_map/all_gather | solution.py:101
  89.5 56.1 %copy-start.2 = (bf16[128,1536]{1,0:T(8,128)(2,1)S(1)}, bf16[128,1536]{1,0:T(8,128)(2,1)}, u32[]{:S(2)}) copy-start(bf16[128,1536]{1,0:T(8,128)(2,1)} %param.12) | copy-start | bytes 1179652
  145.5 137.3 %all-gather.13.cloned.1.call-start = ((), (), s32[]{:S(2)}) async-start(), calls=%async_computation.13 | async-start | bytes 1966080 | tf_op jit(solution)/shard_map/all_gather | solution.py:135
  146.8 263.4 %copy-start.25 = (f32[128]{0:T(128)}, f32[128]{0:T(128)S(1)}, u32[]{:S(2)}) copy-start(f32[128]{0:T(128)S(1)} %add_rsqrt_fusion) | copy-start | bytes 1540
  148.8 171.5 %all-gather.15.cloned.1.call-start = ((), (), s32[]{:S(2)}) async-start(), calls=%async_computation.15 | async-start | bytes 1966080 | tf_op jit(solution)/shard_map/all_gather | solution.py:134
  332.9 8.8 all-to-all-start.1
  336.1 72.6 %reduce-scatter.14.cloned.1.call-start = ((), (), s32[]{:S(2)}) async-start(), calls=%async_computation.16 | async-start | bytes 1966080 | tf_op jit(solution)/shard_map/reduce_scatter | solution.py:152
  364.2 44.5 %copy-start.3 = (bf16[128,1536]{1,0:T(8,128)(2,1)S(1)}, bf16[128,1536]{1,0:T(8,128)(2,1)}, u32[]{:S(2)}) copy-start(bf16[128,1536]{1,0:T(8,128)(2,1)} %reduce-scatter.10.cloned.1.call-done) | copy-start | bytes 1179652
  375.1 36.0 %copy-start.7 = (bf16[128,1536]{1,0:T(8,128)(2,1)S(1)}, bf16[128,1536]{1,0:T(8,128)(2,1)}, u32[]{:S(2)}) copy-start(bf16[128,1536]{1,0:T(8,128)(2,1)} %param.23) | copy-start | bytes 1179652
  375.1 68.5 %all-gather.17.cloned.1.call-start = ((), (), s32[]{:S(2)}) async-start(), calls=%async_computation.17 | async-start | bytes 3538944 | tf_op jit(solution)/shard_map/all_gather | solution.py:181
  410.2 36.5 %copy-start.31 = (f32[128]{0:T(128)}, f32[128]{0:T(128)S(1)}, u32[]{:S(2)}) copy-start(f32[128]{0:T(128)S(1)} %broadcast_multiply_fusion.1) | copy-start | bytes 1540
  412.2 34.6 %copy-start.23 = (f32[8,3,128]{2,1,0:T(4,128)S(1)}, f32[8,3,128]{2,1,0:T(4,128)}, u32[]{:S(2)}) copy-start(f32[8,3,128]{2,1,0:T(4,128)} %copy-done.22) | copy-start | bytes 36868
  412.2 154.8 %reduce-scatter.16.cloned.1.call-start = ((), (), s32[]{:S(2)}) async-start(), calls=%async_computation.18 | async-start | bytes 3538944 | tf_op jit(solution)/shard_map/reduce_scatter | solution.py:196
  454.7 115.1 %reduce-scatter.22.cloned.1.call-start = ((), (), s32[]{:S(2)}) async-start(), calls=%async_computation.26 | async-start | bytes 1474560
  461.4 110.4 %all-reduce.6.cloned.1.call-start = ((), (), s32[]{:S(2)}) async-start(), calls=%async_computation.20 | async-start | bytes 1179648 | tf_op jit(solution)/shard_map/psum | solution.py:205
  461.6 7.0 copy-start.13
  468.6 10.6 %copy-start.9 = (bf16[1024,1536]{1,0:T(8,128)(2,1)S(1)}, bf16[1024,1536]{1,0:T(8,128)(2,1)}, u32[]{:S(2)}) copy-start(bf16[1024,1536]{1,0:T(8,128)(2,1)} %all-gather.17.cloned.1.call-done) | copy-start | bytes 9437188
  480.9 203.3 %reduce-scatter.20.cloned.1.call-start = ((), (), s32[]{:S(2)}) async-start(), calls=%async_computation.22 | async-start | bytes 21233664 | tf_op jit(solution)/shard_map/reduce_scatter | solution.py:160
  557.8 9.0 copy-start.6
  557.8 9.2 copy-start.19
  557.9 9.2 copy-start.28
  557.9 216.0 %reduce-scatter.12.cloned.1.call-start = ((), (), s32[]{:S(2)}) async-start(), calls=%async_computation.14 | async-start | bytes 1966080 | tf_op jit(solution)/shard_map/reduce_scatter | solution.py:167
  566.8 213.1 %reduce-scatter.18.cloned.1.call-start = ((), (), s32[]{:S(2)}) async-start(), calls=%async_computation.19 | async-start | bytes 184320 | tf_op jit(solution)/shard_map/reduce_scatter | solution.py:222
  569.7 238.7 %all-gather.25.cloned.1.call-start = ((), (), s32[]{:S(2)}) async-start(), calls=%async_computation.25 | async-start | bytes 2211840 | tf_op jit(solution)/shard_map/all_gather | solution.py:210
  571.7 277.7 %all-gather.19.cloned.1.call-start = ((), (), s32[]{:S(2)}) async-start(), calls=%async_computation.21 | async-start | bytes 5308416 | tf_op jit(solution)/shard_map/all_gather | solution.py:219
  572.4 378.2 %all-gather.21.cloned.1.call-start = ((), (), s32[]{:S(2)}) async-start(), calls=%async_computation.23 | async-start | bytes 21233664 | tf_op jit(solution)/shard_map/all_gather | solution.py:164
  984.0 29.1 %copy-start.1 = (bf16[384,1536]{1,0:T(8,128)(2,1)S(1)}, bf16[384,1536]{1,0:T(8,128)(2,1)}, u32[]{:S(2)}) copy-start(bf16[384,1536]{1,0:T(8,128)(2,1)} %param.15) | copy-start | bytes 3538948
  (22 other events, 60.6 us)
Sparse Core Ops, SparseCore 0:
  28.4 33.5 all-gather.10
  85.3 46.5 reduce-scatter.9
  145.7 97.9 all-gather.22
  245.7 37.0 all-gather.12
  284.3 35.9 all-gather.14
  412.3 31.1 all-gather.16
  454.8 46.2 reduce-scatter.15
  503.4 35.9 reduce-scatter.21
  558.0 126.1 reduce-scatter.19
  686.9 60.2 reduce-scatter.11
  750.0 29.9 reduce-scatter.17
  782.4 26.0 all-gather.24
  810.5 38.8 all-gather.18
  851.9 98.7 all-gather.20
Sparse Core Ops, SparseCore 1:
  31.7 48.7 all-reduce.3
  375.2 33.5 reduce-scatter.13
  480.9 51.6 all-reduce.5
where the time goes:
time: 1030 us; the launch traced here: 1020 us
  waiting for transfers between devices  454 us (44%)
  blocking collectives  230 us (22%)
  local copies, waits for them, and re-layouts  154 us (15%)
  matrix products  89.6 us (9%)
  other arithmetic  70.9 us (7%)
  between operations  17.6 us (2%)
    reduce_scatter x1, waiting for transfers between devices, shards(): gw = lax.psum_scatter(gw, 'rep', scatter_dimension=0, tiled=True)  111 us
    all_gather x1, waiting for transfers between devices, shards(): gw = lax.all_gather(gw, 'rep', axis=0, tiled=True)  98.3 us
    all_gather x1, waiting for transfers between devices, shards(): both = lax.all_gather(both, 'rep', axis=0, tiled=False)  88.9 us
    all_to_all x1, blocking collectives, shards(): gw = lax.all_to_all(gw, 'grp', 0, 0, tiled=True)  84.3 us
    unnamed x85, local copies, waits for them, and re-layouts  72.8 us
    all_to_all x1, blocking collectives, shards(): both = lax.all_to_all(both, 'grp', 0, 0, tiled=True)  56 us
    reduce_scatter x1, waiting for transfers between devices, shards(): lax.psum_scatter(gact_part, 'grp', scatter_dimension=0, tiled=True)  33.6 us
    all_gather x1, waiting for transfers between devices, shards(): lax.all_gather(gres_low, 'rep', axis=0, tiled=True, axis_index_groups=gro...  31.3 us
  transfers between devices with their start and end apart: 18, of which 11 were waited for; matrix products, arithmetic and copies ran while one was open for 19% of the time, Pallas kernels for 0%

commit v1 on v0

--- a/solution.py
+++ b/solution.py
@@ -14,6 +14,29 @@
 F32 = jnp.float32
 QPK = QUERY_HEADS // KEY_VALUE_HEADS
 BIG = 1 << 20
+
+
+def in_blocks(x, dim, size):
+    lengths = x.shape
+    blocks = x.reshape(*lengths[:dim], size, lengths[dim] // size, *lengths[dim + 1 :])
+    return jnp.moveaxis(blocks, dim, 0)
+
+
+def laid_out(blocks, dim):
+    blocks = jnp.moveaxis(blocks, 0, dim)
+    shape = blocks.shape
+    return blocks.reshape(*shape[:dim], shape[dim] * shape[dim + 1], *shape[dim + 2 :])
+
+
+def pairwise_exchange(x, axis, split_dim, concat_dim):
+    devices, position = (lax.axis_size(axis), lax.axis_index(axis))
+    blocks = in_blocks(x, split_dim, devices)
+    finished = [blocks[position]]
+    for step in range(1, devices):
+        sent = blocks[position ^ step]
+        finished.append(lax.ppermute(sent, axis, [(i, i ^ step) for i in range(devices)]))
+    blocks = jnp.stack(finished)[position ^ jnp.arange(devices)]
+    return laid_out(blocks, concat_dim)
 
 
 def dot(a, b):
@@ -159,7 +182,7 @@
     gw = gw.reshape(reps * grps * piece, EXPERTS // grps * 3 * HID)
     gw = lax.psum_scatter(gw, "rep", scatter_dimension=0, tiled=True)
     gw = gw.reshape(grps, piece, local_experts, 3 * HID)
-    gw = lax.all_to_all(gw, "grp", 0, 0, tiled=True)
+    gw = pairwise_exchange(gw, "grp", 0, 0)
     gw = gw.transpose(1, 0, 2, 3).reshape(piece, EXPERTS, 3 * HID)
     gw = lax.all_gather(gw, "rep", axis=0, tiled=True)
     grad_gu = gw[:, :, : 2 * HID].astype(F32)

time: 1030 us -> 991 us (0.962)
  blocking collectives: 230 us -> 146 us
  waiting for transfers between devices: 454 us -> 529 us
  local copies, waits for them, and re-layouts: 154 us -> 112 us
    all_to_all x1 -> x0, blocking collectives: 84.3 us -> none  [shards(): gw = lax.all_to_all(gw, 'grp', 0, 0, tiled=True)]
    ppermute x0 -> x3, waiting for transfers between devices: none -> 63.8 us  [pairwise_exchange(): lax.ppermute(sent, axis, [(i, i ^ step) for i in range(devices)])]
    unnamed x85 -> x84, local copies, waits for them, and re-layouts: 72.8 us -> 27.1 us
  transfers between devices with their start and end apart: 18 -> 21, of which waited for: 11 -> 13; matrix products, arithmetic and copies ran while one was open for 19% -> 20% of each run, Pallas kernels for 0% -> 0%
where the time goes in v1:
time: 991 us; the launch traced here: 982 us
  waiting for transfers between devices  529 us (53%)
  blocking collectives  146 us (15%)
  local copies, waits for them, and re-layouts  112 us (11%)
  matrix products  89.7 us (9%)
  other arithmetic  78.2 us (8%)
  between operations  17.4 us (2%)
    reduce_scatter x1, waiting for transfers between devices, shards(): gw = lax.psum_scatter(gw, 'rep', scatter_dimension=0, tiled=True)  113 us
    all_gather x1, waiting for transfers between devices, shards(): gw = lax.all_gather(gw, 'rep', axis=0, tiled=True)  98.3 us
    all_gather x1, waiting for transfers between devices, shards(): both = lax.all_gather(both, 'rep', axis=0, tiled=False)  88.9 us
    ppermute x3, waiting for transfers between devices, pairwise_exchange(): lax.ppermute(sent, axis, [(i, i ^ step) for i in range(devices)])  63.8 us
    all_to_all x1, blocking collectives, shards(): both = lax.all_to_all(both, 'grp', 0, 0, tiled=True)  56 us
    reduce_scatter x1, waiting for transfers between devices, shards(): lax.psum_scatter(gact_part, 'grp', scatter_dimension=0, tiled=True)  33.6 us
    all_gather x1, waiting for transfers between devices, shards(): lax.all_gather(gres_low, 'rep', axis=0, tiled=True, axis_index_groups=gro...  31.3 us
    all_gather x1, blocking collectives, shards(): qkv_head = lax.all_gather(qkv_cols, 'grp', axis=0, tiled=True)  30.3 us
  transfers between devices with their start and end apart: 21, of which 13 were waited for; matrix products, arithmetic and copies ran while one was open for 20% of the time, Pallas kernels for 0%

profile of v1, /device:TPU:0, one launch (start us, length us, event | category | flops | bytes accessed | tf_op | source)
XLA Modules:
  0.0 981.8 jit_solution(3075821671703443079)
XLA Ops:
  11.4 14.9 %all_gather.42 = bf16[1536,18]{0,1:T(8,128)(2,1)S(1)} all-gather(bf16[384,18]{0,1:T(8,128)(2,1)S(1)} %pad_maximum_fusion.17), channel_id=1, replica_groups=mesh['rep'=8,'grp'=4] {'grp'}, dimensions={0}, use_global_device_ids=true | all-gather | bytes 69120 | tf_op jit(solution)/shard_map/all_gather | solution.py:100
  32.6 8.0 all-reduce
  43.2 30.3 %all_gather.44 = bf16[1536,320]{1,0:T(8,128)(2,1)S(1)} all-gather(bf16[384,320]{1,0:T(8,128)(2,1)S(1)} %pad_maximum_fusion.9), channel_id=1, replica_groups=mesh['rep'=8,'grp'=4] {'grp'}, dimensions={0}, use_global_device_ids=true | all-gather | bytes 1228800 | tf_op jit(solution)/shard_map/all_gather | solution.py:111
  89.5 56.0 %all_to_all.24 = bf16[4,4,48,1536]{3,2,1,0:T(8,128)(2,1)} all-to-all(bf16[4,4,48,1536]{3,2,1,0:T(8,128)(2,1)S(1)} %bitcast.210), channel_id=1, replica_groups=mesh['rep'=8,'grp'=4] {'grp'}, dimensions={0} | all-to-all | bytes 4718592 | tf_op jit(solution)/shard_map/all_to_all | solution.py:123
  154.7 88.9 %all-gather.23.cloned.1.call-done = bf16[32,4,48,1536]{3,2,1,0:T(8,128)(2,1)} async-done(((bf16[4,4,48,1536]{3,2,1,0:T(8,128)(2,1)}), bf16[32,4,48,1536]{3,2,1,0:T(8,128)(2,1)}) %all-gather.23.cloned.1.call-update) | async-done | bytes 18874384 | tf_op jit(solution)/shard_map/all_gather | solution.py:124
  243.6 17.1 %copy.167 = bf16[4,4,8,48,1536]{4,3,2,1,0:T(8,128)(2,1)} copy(bf16[4,4,8,48,1536]{4,3,0,1,2:T(8,128)(2,1)} %bitcast.205) | data formatting | bytes 37748736 | tf_op jit(solution)/shard_map/transpose | solution.py:125
  260.8 22.1 %all-gather.13.cloned.1.call-done = bf16[512,1536]{1,0:T(8,128)(2,1)} async-done(((bf16[128,1536]{1,0:T(8,128)(2,1)}), bf16[512,1536]{1,0:T(8,128)(2,1)}) %all-gather.13.cloned.1.call-update) | async-done | bytes 1572880 | tf_op jit(solution)/shard_map/all_gather | solution.py:158
  282.9 12.3 %fusion.18 = f32[4,512,1024]{1,2,0:T(8,128)} fusion(bf16[4,1536,1536]{2,1,0:T(8,128)(2,1)} %bitcast.201, bf16[512,1536]{1,0:T(8,128)(2,1)} %all-gather.13.cloned.1.call-done), kind=kOutput, calls=%fused_computation.32 | convolution fusion | flops 6442450944 | bytes 22544384 | tf_op jit(solution)/shard_map/td,edh->eth/dot_general | solution.py:161
  295.2 25.2 %all-gather.15.cloned.1.call-done = bf16[512,1536]{1,0:T(8,128)(2,1)} async-done(((bf16[128,1536]{1,0:T(8,128)(2,1)}), bf16[512,1536]{1,0:T(8,128)(2,1)}) %all-gather.15.cloned.1.call-update) | async-done | bytes 1572880 | tf_op jit(solution)/shard_map/all_gather | solution.py:157
  320.3 12.6 %fusion.10 = (f32[4,512]{1,0:T(4,128)}, f32[4,512,512]{2,1,0:T(8,128)}) fusion(f32[4,512,1024]{1,2,0:T(8,128)} %fusion.18, bf16[512,1536]{1,0:T(8,128)(2,1)} %all-gather.15.cloned.1.call-done, bf16[4,1536,1536]{2,1,0:T(8,128)(2,1)} %bitcast.202), kind=kOutput, calls=%fused_computation.20 | convolution fusion | flops 3228563456 | bytes 20455424 | tf_op jit(solution)/shard_map/td,edh->eth/dot_general | solution.py:167
  341.8 13.3 %all_gather.49 = f32[512,16]{0,1:T(8,128)S(1)} all-gather(f32[128,16]{0,1:T(8,128)S(1)} %get-tuple-element.84), channel_id=1, replica_groups=mesh['rep'=8,'grp'=4] {'grp'}, dimensions={0}, use_global_device_ids=true | all-gather | bytes 40960 | tf_op jit(solution)/shard_map/all_gather | solution.py:159
  355.1 6.9 multiply_convert_fusion.1
  364.1 10.8 %fusion.24 = bf16[512,1536]{1,0:T(8,128)(2,1)} fusion(bf16[4,1536,1536]{2,1,0:T(8,128)(2,1)} %bitcast.203, bf16[4,512,512]{1,2,0:T(8,128)(2,1)S(1)} %get-tuple-element.65, bf16[4,512,512]{1,2,0:T(8,128)(2,1)S(1)} %get-tuple-element.64), kind=kOutput, calls=%fused_computation.34 | convolution fusion | flops 6451625984 | bytes 18350080 | tf_op jit(solution)/shard_map/eth,edh->td/dot_general | solution.py:174
  375.0 33.6 %reduce-scatter.14.cloned.1.call-done = bf16[128,1536]{1,0:T(8,128)(2,1)} async-done(((bf16[512,1536]{1,0:T(8,128)(2,1)}), bf16[128,1536]{1,0:T(8,128)(2,1)}) %reduce-scatter.14.cloned.1.call-update) | async-done | bytes 393232 | tf_op jit(solution)/shard_map/reduce_scatter | solution.py:175
  412.1 31.3 %all-gather.17.cloned.1.call-done = bf16[1024,1536]{1,0:T(8,128)(2,1)} async-done(((bf16[128,1536]{1,0:T(8,128)(2,1)}), bf16[1024,1536]{1,0:T(8,128)(2,1)}) %all-gather.17.cloned.1.call-update) | async-done | bytes 3145744 | tf_op jit(solution)/shard_map/all_gather | solution.py:204
  461.7 7.0 convert_bitcast_fusion
  468.7 10.6 %fusion.5 = bf16[4,1536,1024]{1,2,0:T(8,128)(2,1)} fusion(bf16[4,512,512]{1,2,0:T(8,128)(2,1)S(1)} %copy-done.15, bf16[4,512,512]{1,2,0:T(8,128)(2,1)S(1)} %copy-done.13, bf16[512,1536]{1,0:T(8,128)(2,1)S(1)} %copy-done.34), kind=kOutput, calls=%fused_computation.10 | convolution fusion | flops 6457131008 | bytes 18350080 | tf_op jit(solution)/shard_map/td,eth->edh/dot_general | solution.py:178
  481.0 20.9 %pad_maximum_fusion = bf16[4,1536,1536]{1,2,0:T(8,128)(2,1)} fusion(bf16[4,1536,512]{1,2,0:T(8,128)(2,1)} %convert_bitcast_fusion, bf16[4,1536,1024]{1,2,0:T(8,128)(2,1)} %fusion.5), kind=kLoop, calls=%fused_computation.3 | loop fusion | flops 37748736 | bytes 37748736 | tf_op jit(solution)/shard_map/concatenate | solution.py:180
  502.0 23.2 %copy.185 = bf16[4,1536,1536]{2,1,0:T(8,128)(2,1)} copy(bf16[4,1536,1536]{1,2,0:T(8,128)(2,1)} %pad_maximum_fusion) | data formatting | bytes 37748736 | tf_op jit(solution)/shard_map/concatenate | solution.py:180
  525.1 21.6 %copy.186 = bf16[8,4,48,4,1536]{4,3,2,1,0:T(4,128)(2,1)S(1)} copy(bf16[8,4,48,4,1536]{4,2,0,1,3:T(8,128)(2,1)} %bitcast.199) | data formatting | bytes 37748736 | tf_op jit(solution)/shard_map/transpose | solution.py:181
  546.7 9.7 copy.217
  558.0 7.4 fusion.21
  571.2 112.9 %reduce-scatter.20.cloned.1.call-done = bf16[192,6144]{1,0:T(8,128)(2,1)} async-done(((bf16[1536,6144]{1,0:T(8,128)(2,1)}), bf16[192,6144]{1,0:T(8,128)(2,1)}) %reduce-scatter.20.cloned.1.call-update) | async-done | bytes 2359312 | tf_op jit(solution)/shard_map/reduce_scatter | solution.py:183
  693.4 44.3 %collective-permute-done = bf16[1,48,4,1536]{3,1,2,0:T(8,128)(2,1)S(1)} collective-permute-done((bf16[1,48,4,1536]{3,1,2,0:T(8,128)(2,1)S(1)}, bf16[1,48,4,1536]{3,1,2,0:T(8,128)(2,1)S(1)}, u32[]{:S(2)}, u32[]{:S(2)}) %collective-permute-start) | collective-permute-done | bytes 589856 | tf_op jit(solution)/shard_map/ppermute | solution.py:37
  737.8 19.5 %collective-permute-done.1 = bf16[1,48,4,1536]{3,1,2,0:T(8,128)(2,1)S(1)} collective-permute-done((bf16[1,48,4,1536]{3,1,2,0:T(8,128)(2,1)S(1)}, bf16[1,48,4,1536]{3,1,2,0:T(8,128)(2,1)S(1)}, u32[]{:S(2)}, u32[]{:S(2)}) %collective-permute-start.1) | collective-permute-done | bytes 589856 | tf_op jit(solution)/shard_map/ppermute | solution.py:37
  766.9 12.9 %reduce-scatter.18.cloned.1.call-done = f32[384,18]{0,1:T(8,128)} async-done(((f32[1536,18]{0,1:T(8,128)}), f32[384,18]{0,1:T(8,128)}) %reduce-scatter.18.cloned.1.call-update) | async-done | bytes 27664 | tf_op jit(solution)/shard_map/reduce_scatter | solution.py:245
  779.8 23.5 %psum.22 = f32[384,18]{0,1:T(8,128)S(1)} all-reduce(f32[384,18]{0,1:T(8,128)} %reduce-scatter.18.cloned.1.call-done), channel_id=1, replica_groups=mesh['rep'=8,'grp'=4] {'rep'}, use_global_device_ids=true, to_apply=%region_22.23 | all-reduce | flops 6912 | bytes 55296 | tf_op jit(solution)/shard_map/psum | solution.py:245
  814.3 5.5 copy.192
  819.8 29.4 %all-gather.19.cloned.1.call-done = bf16[1536,1536]{1,0:T(8,128)(2,1)} async-done(((bf16[192,1536]{1,0:T(8,128)(2,1)}), bf16[1536,1536]{1,0:T(8,128)(2,1)}) %all-gather.19.cloned.1.call-update) | async-done | bytes 4718608 | tf_op jit(solution)/shard_map/all_gather | solution.py:242
  852.2 98.3 %all-gather.21.cloned.1.call-done = bf16[384,16,1536]{2,1,0:T(8,128)(2,1)} async-done(((bf16[48,16,1536]{2,1,0:T(8,128)(2,1)}), bf16[384,16,1536]{2,1,0:T(8,128)(2,1)}) %all-gather.21.cloned.1.call-update) | async-done | bytes 18874384 | tf_op jit(solution)/shard_map/all_gather | solution.py:187
  950.5 9.3 slice_convert_fusion.1
  959.8 14.4 %slice_convert_fusion = f32[384,16,1024]{2,1,0:T(8,128)} fusion(bf16[384,16,1536]{2,1,0:T(8,128)(2,1)} %all-gather.21.cloned.1.call-done), kind=kLoop, calls=%fused_computation.5 | loop fusion | flops 6291456 | bytes 37748736 | tf_op jit(solution)/shard_map/convert_element_type | solution.py:188
  (221 shorter events, 110.6 us)
Async XLA Ops:
  8.0 20.4 %copy-start = (bf16[384,1536]{1,0:T(8,128)(2,1)S(1)}, bf16[384,1536]{1,0:T(8,128)(2,1)}, u32[]{:S(2)}) copy-start(bf16[384,1536]{1,0:T(8,128)(2,1)} %param.15) | copy-start | bytes 3538948
  8.0 65.7 %all-gather.11.cloned.1.call-start = ((), (), s32[]{:S(2)}) async-start(), calls=%async_computation.9 | async-start | bytes 3538944 | tf_op jit(solution)/shard_map/all_gather | solution.py:131
  9.3 19.0 %copy-start.27 = (f32[128]{0:T(128)}, f32[128]{0:T(128)S(1)}, u32[]{:S(2)}) copy-start(f32[128]{0:T(128)S(1)} %add_rsqrt_fusion.1) | copy-start | bytes 1540
  28.3 53.1 %all-reduce.4.cloned.1.call-start = ((), (), s32[]{:S(2)}) async-start(), calls=%async_computation.10 | async-start | bytes 1179648 | tf_op jit(solution)/shard_map/psum | solution.py:117
  30.5 115.1 %reduce-scatter.10.cloned.1.call-start = ((), (), s32[]{:S(2)}) async-start(), calls=%async_computation.11 | async-start | bytes 3538944 | tf_op jit(solution)/shard_map/reduce_scatter | solution.py:151
  85.2 158.4 %all-gather.23.cloned.1.call-start = ((), (), s32[]{:S(2)}) async-start(), calls=%async_computation.23 | async-start | bytes 21233664 | tf_op jit(solution)/shard_map/all_gather | solution.py:124
  89.5 56.1 %copy-start.2 = (bf16[128,1536]{1,0:T(8,128)(2,1)S(1)}, bf16[128,1536]{1,0:T(8,128)(2,1)}, u32[]{:S(2)}) copy-start(bf16[128,1536]{1,0:T(8,128)(2,1)} %param.12) | copy-start | bytes 1179652
  145.6 137.3 %all-gather.13.cloned.1.call-start = ((), (), s32[]{:S(2)}) async-start(), calls=%async_computation.12 | async-start | bytes 1966080 | tf_op jit(solution)/shard_map/all_gather | solution.py:158
  146.9 263.2 %copy-start.25 = (f32[128]{0:T(128)}, f32[128]{0:T(128)S(1)}, u32[]{:S(2)}) copy-start(f32[128]{0:T(128)S(1)} %add_rsqrt_fusion) | copy-start | bytes 1540
  148.8 171.5 %all-gather.15.cloned.1.call-start = ((), (), s32[]{:S(2)}) async-start(), calls=%async_computation.14 | async-start | bytes 1966080 | tf_op jit(solution)/shard_map/all_gather | solution.py:157
  332.9 8.8 all-to-all-start.1
  336.2 72.4 %reduce-scatter.14.cloned.1.call-start = ((), (), s32[]{:S(2)}) async-start(), calls=%async_computation.15 | async-start | bytes 1966080 | tf_op jit(solution)/shard_map/reduce_scatter | solution.py:175
  364.1 44.5 %copy-start.3 = (bf16[128,1536]{1,0:T(8,128)(2,1)S(1)}, bf16[128,1536]{1,0:T(8,128)(2,1)}, u32[]{:S(2)}) copy-start(bf16[128,1536]{1,0:T(8,128)(2,1)} %reduce-scatter.10.cloned.1.call-done) | copy-start | bytes 1179652
  374.9 36.0 %copy-start.7 = (bf16[128,1536]{1,0:T(8,128)(2,1)S(1)}, bf16[128,1536]{1,0:T(8,128)(2,1)}, u32[]{:S(2)}) copy-start(bf16[128,1536]{1,0:T(8,128)(2,1)} %param.23) | copy-start | bytes 1179652
  374.9 68.5 %all-gather.17.cloned.1.call-start = ((), (), s32[]{:S(2)}) async-start(), calls=%async_computation.16 | async-start | bytes 3538944 | tf_op jit(solution)/shard_map/all_gather | solution.py:204
  410.1 36.5 %copy-start.31 = (f32[128]{0:T(128)}, f32[128]{0:T(128)S(1)}, u32[]{:S(2)}) copy-start(f32[128]{0:T(128)S(1)} %broadcast_multiply_fusion.1) | copy-start | bytes 1540
  412.0 34.6 %copy-start.23 = (f32[8,3,128]{2,1,0:T(4,128)S(1)}, f32[8,3,128]{2,1,0:T(4,128)}, u32[]{:S(2)}) copy-start(f32[8,3,128]{2,1,0:T(4,128)} %copy-done.22) | copy-start | bytes 36868
  412.1 153.6 %reduce-scatter.16.cloned.1.call-start = ((), (), s32[]{:S(2)}) async-start(), calls=%async_computation.17 | async-start | bytes 3538944 | tf_op jit(solution)/shard_map/reduce_scatter | solution.py:219
  454.5 113.8 %reduce-scatter.22.cloned.1.call-start = ((), (), s32[]{:S(2)}) async-start(), calls=%async_computation.25 | async-start | bytes 1474560
  461.2 109.1 %all-reduce.6.cloned.1.call-start = ((), (), s32[]{:S(2)}) async-start(), calls=%async_computation.19 | async-start | bytes 1179648 | tf_op jit(solution)/shard_map/psum | solution.py:228
  468.7 10.6 %copy-start.9 = (bf16[1024,1536]{1,0:T(8,128)(2,1)S(1)}, bf16[1024,1536]{1,0:T(8,128)(2,1)}, u32[]{:S(2)}) copy-start(bf16[1024,1536]{1,0:T(8,128)(2,1)} %all-gather.17.cloned.1.call-done) | copy-start | bytes 9437188
  481.0 203.2 %reduce-scatter.20.cloned.1.call-start = ((), (), s32[]{:S(2)}) async-start(), calls=%async_computation.21 | async-start | bytes 21233664 | tf_op jit(solution)/shard_map/reduce_scatter | solution.py:183
  556.4 9.2 copy-start.19
  556.4 207.8 %reduce-scatter.12.cloned.1.call-start = ((), (), s32[]{:S(2)}) async-start(), calls=%async_computation.13 | async-start | bytes 1966080 | tf_op jit(solution)/shard_map/reduce_scatter | solution.py:190
  565.4 214.4 %reduce-scatter.18.cloned.1.call-start = ((), (), s32[]{:S(2)}) async-start(), calls=%async_computation.18 | async-start | bytes 184320 | tf_op jit(solution)/shard_map/reduce_scatter | solution.py:245
  568.3 240.0 %all-gather.25.cloned.1.call-start = ((), (), s32[]{:S(2)}) async-start(), calls=%async_computation.24 | async-start | bytes 2211840 | tf_op jit(solution)/shard_map/all_gather | solution.py:233
  570.3 279.0 %all-gather.19.cloned.1.call-start = ((), (), s32[]{:S(2)}) async-start(), calls=%async_computation.20 | async-start | bytes 5308416 | tf_op jit(solution)/shard_map/all_gather | solution.py:242
  571.0 379.5 %all-gather.21.cloned.1.call-start = ((), (), s32[]{:S(2)}) async-start(), calls=%async_computation.22 | async-start | bytes 21233664 | tf_op jit(solution)/shard_map/all_gather | solution.py:187
  688.9 48.9 %collective-permute-start = (bf16[1,48,4,1536]{3,1,2,0:T(8,128)(2,1)S(1)}, bf16[1,48,4,1536]{3,1,2,0:T(8,128)(2,1)S(1)}, u32[]{:S(2)}, u32[]{:S(2)}) collective-permute-start(bf16[1,48,4,1536]{3,1,2,0:T(8,128)(2,1)S(1)} %bitcast.225), channel_id=1, source_target_pairs={{0,1},{1,0},{2,3},{3,2},{4,5},{5,4},{6,7},{7,6},{8,9},{9,8},{10,11... | collective-permute-start | bytes 1769480 | tf_op jit(solution)/shard_map/ppermute | solution.py:37
  690.4 66.9 %collective-permute-start.1 = (bf16[1,48,4,1536]{3,1,2,0:T(8,128)(2,1)S(1)}, bf16[1,48,4,1536]{3,1,2,0:T(8,128)(2,1)S(1)}, u32[]{:S(2)}, u32[]{:S(2)}) collective-permute-start(bf16[1,48,4,1536]{3,1,2,0:T(8,128)(2,1)S(1)} %bitcast.224), channel_id=1, source_target_pairs={{0,2},{1,3},{2,0},{3,1},{4,6},{5,7},{6,4},{7,5},{8,10},{9,11},{10,... | collective-permute-start | bytes 1769480 | tf_op jit(solution)/shard_map/ppermute | solution.py:37
  692.8 64.5 %collective-permute-start.2 = (bf16[1,48,4,1536]{3,1,2,0:T(8,128)(2,1)S(1)}, bf16[1,48,4,1536]{3,1,2,0:T(8,128)(2,1)S(1)}, u32[]{:S(2)}, u32[]{:S(2)}) collective-permute-start(bf16[1,48,4,1536]{3,1,2,0:T(8,128)(2,1)S(1)} %bitcast.223), channel_id=1, source_target_pairs={{0,3},{1,2},{2,1},{3,0},{4,7},{5,6},{6,5},{7,4},{8,11},{9,10},{10,... | collective-permute-start | bytes 1769480 | tf_op jit(solution)/shard_map/ppermute | solution.py:37
  959.8 14.4 %copy-start.1 = (bf16[384,1536]{1,0:T(8,128)(2,1)S(1)}, bf16[384,1536]{1,0:T(8,128)(2,1)}, u32[]{:S(2)}) copy-start(bf16[384,1536]{1,0:T(8,128)(2,1)} %param.15) | copy-start | bytes 3538948
  (25 other events, 104.5 us)
Sparse Core Ops, SparseCore 0:
  28.4 33.5 all-gather.10
  85.3 46.4 reduce-scatter.9
  145.7 97.9 all-gather.22
  245.7 37.0 all-gather.12
  284.3 35.9 all-gather.14
  412.2 31.1 all-gather.16
  454.7 46.2 reduce-scatter.15
  503.3 36.3 reduce-scatter.21
  556.5 127.6 reduce-scatter.19
  686.9 59.3 reduce-scatter.11
  748.6 31.1 reduce-scatter.17
  782.3 25.9 all-gather.24
  810.3 38.8 all-gather.18
  851.7 98.7 all-gather.20
Sparse Core Ops, SparseCore 1:
  31.7 48.7 all-reduce.3
  375.0 33.5 reduce-scatter.13
  481.1 51.5 all-reduce.5
